TPU v7x, 32 devices: a whole 2x2x4 slice. The times are simulated.
32 devices in a mesh: ctx: 16 (over z, y, core), ch: 2 (over x).
Axes of the slice: x: 2, y: 2, z: 4, core: 2. Of those that a mesh axis runs over, the one named last changes fastest.
Arguments:
- activations: bfloat16 [2, 2048, 8192], P(None, 'ctx', 'ch'), may hold values from -62 to 62
- grad_in: bfloat16 [2, 2048, 8192], P(None, 'ctx', 'ch'), may hold values from -6 to 6
- gate_out: bfloat16 [3, 2, 2048, 8192], P(None, None, 'ctx', 'ch'), may hold values from -6 to 6
- gate_in: bfloat16 [3, 2, 2048, 8192], P(None, None, 'ctx', 'ch'), may hold values from -6 to 6
- filters: bfloat16 [3, 512, 128], P(None, 'ch'), may hold values from -0.5 to 0.5
Outputs:
- grad_input: bfloat16 [2, 2048, 8192], P(None, 'ctx', 'ch')
- grad_gate_out: bfloat16 [3, 2, 2048, 8192], P(None, None, 'ctx', 'ch')
- grad_gate_in: bfloat16 [3, 2, 2048, 8192], P(None, None, 'ctx', 'ch')
- grad_filters: float32 [3, 512, 128], P(None, 'ch', 'ctx')
All inputs are finite; a program needn't handle non-finite values.
Results may differ from a plain program's by a relative error of at most 0.023.
Values may be sent and summed in bfloat16 or wider, within the bound.
No kernel may reach another device: no remote copies, remote signals or barrier semaphores. Data moves between devices by JAX's collectives and lax.ppermute only.
A program may use at most 256 MiB of HBM per device.

v0:
```python
import functools

import jax
import jax.numpy as jnp
from jax import lax
from jax.experimental import pallas as pl
from jax.experimental.pallas import tpu as pltpu
from jax.sharding import PartitionSpec as P

D = 8192
GROUP = 16
LAYERS = 3
EPS = 1e-06
LANES = 128
SUB = 8
BLOCK = 1024
HEIGHT = 32
VMEM_LIMIT = 20 * 1024 * 1024

f32 = jnp.float32
bf16 = jnp.bfloat16


def down_rows(row):
    count = row.shape[1]
    return jnp.broadcast_to(row, (count, count)).T


def lane_sums(acc):
    return jnp.broadcast_to(jnp.sum(acc.T, axis=0, keepdims=True), (SUB, acc.shape[0]))


def lag_flip(taps):
    row = lax.broadcasted_iota(jnp.int32, (taps, taps), 0)
    col = lax.broadcasted_iota(jnp.int32, (taps, taps), 1)
    return (lax.rem(row + col, taps) == 0).astype(bf16)


def band_masks(height, taps, behind):
    row = lax.broadcasted_iota(jnp.int32, (height, taps), 0)
    col = lax.broadcasted_iota(jnp.int32, (height, taps), 1)
    first = (col > row) if behind else (col >= row)
    return jnp.concatenate(
        [jnp.where(first, 1.0, 0.0), jnp.where(first, 0.0, 1.0)], axis=1
    ).astype(bf16)


def band(taps_row, masks):
    height, taps = masks.shape[0], taps_row.shape[1]
    wheel = pltpu.roll(
        jnp.broadcast_to(taps_row, (height, taps)), 0, 1, stride=1, stride_axis=0
    ).astype(bf16)
    return jnp.concatenate([wheel, wheel], axis=1) * masks


def windows(signal, height):
    count = signal.shape[0] // 2 // height
    return jnp.concatenate(
        [signal]
        + [
            jnp.concatenate([signal[k * height :], signal[: k * height]], axis=0)
            for k in range(1, count)
        ],
        axis=1,
    )


def group_pick(stacked, height, sides):
    count = LANES // GROUP
    owner = lax.broadcasted_iota(jnp.int32, (height, LANES), 1) // GROUP
    parts = []
    for side in range(sides):
        at = lanes_of(side)
        picked = stacked[:height, at]
        for g in range(1, count):
            picked = jnp.where(owner == g, stacked[g * height : (g + 1) * height, at], picked)
        parts.append(picked)
    return jnp.concatenate(parts, axis=0)


def filtered_block(taps_rows, signal, masks):
    height = masks.shape[0]
    count = LANES // GROUP
    bands = jnp.concatenate([band(taps_rows[g : g + 1], masks) for g in range(count)], axis=0)
    stacked = jnp.dot(bands, windows(signal, height), preferred_element_type=f32)
    return group_pick(stacked, height, signal.shape[0] // 2 // height)


def lanes_of(index):
    return slice(index * LANES, (index + 1) * LANES)


def groups_of(index):
    count = LANES // GROUP
    return slice(index * count, (index + 1) * count)


def scale_of(total_ref):
    return down_rows(lax.rsqrt(total_ref[0:1, :] / D + EPS))


def squares_kernel(x_ref, ssq_ref, acc_ref):
    step = pl.program_id(0)

    @pl.when(step == 0)
    def _():
        acc_ref[...] = jnp.zeros_like(acc_ref)

    for s in range(x_ref.shape[0]):
        for sub in range(x_ref.shape[2] // LANES):
            values = x_ref[s, :, lanes_of(sub)].astype(f32)
            acc_ref[s] += values * values

    @pl.when(step == pl.num_programs(0) - 1)
    def _():
        for s in range(x_ref.shape[0]):
            ssq_ref[s * SUB : (s + 1) * SUB] = lane_sums(acc_ref[s])


def input_kernel(x_ref, tot_ref, gate_ref, *rest):
    u_ref, scale = rest[-2:]

    @pl.when(pl.program_id(0) == 0)
    def _():
        scale[...] = scale_of(tot_ref)

    for sub in range(x_ref.shape[1] // LANES):
        at = lanes_of(sub)
        normed = x_ref[:, at].astype(f32) * scale[...]
        u_ref[:, at] = (gate_ref[:, at].astype(f32) * normed).astype(bf16)


def behind_block(taps, own_ref, halo_ref, sub, masks):
    at = lanes_of(sub)
    signal = jnp.concatenate([halo_ref[:, at], own_ref[:, at]], axis=0)
    return filtered_block(taps[groups_of(sub)], signal, masks)


def flipped_taps(taps_ref):
    return jnp.dot(taps_ref[...], lag_flip(taps_ref.shape[1]), preferred_element_type=f32)


def forward_kernel(taps_ref, own_ref, halo_ref, gate_ref, *rest):
    z_ref, x_ref, ssq_ref, acc_ref = rest[-4:]
    step = pl.program_id(0)

    @pl.when(step == 0)
    def _():
        acc_ref[...] = jnp.zeros_like(acc_ref)

    taps = flipped_taps(taps_ref)
    masks = band_masks(HEIGHT, taps.shape[1], True)
    for sub in range(own_ref.shape[1] // LANES):
        at = lanes_of(sub)
        z = behind_block(taps, own_ref, halo_ref, sub, masks)
        z_ref[:, at] = z.astype(bf16)
        x = (gate_ref[:, at].astype(f32) * z).astype(bf16)
        x_ref[:, at] = x
        values = x.astype(f32)
        acc_ref[...] += values * values

    @pl.when(step == pl.num_programs(0) - 1)
    def _():
        ssq_ref[...] = lane_sums(acc_ref[...])


def last_forward_kernel(taps_ref, own_ref, halo_ref, top_ref, bottom_ref, *rest):
    out_ref = rest[-1]
    taps = flipped_taps(taps_ref)
    masks = band_masks(HEIGHT, taps.shape[1], True)
    for sub in range(own_ref.shape[1] // LANES):
        at = lanes_of(sub)
        z = behind_block(taps, own_ref, halo_ref, sub, masks)
        gradient = jnp.concatenate([top_ref[:, at], bottom_ref[:, at]], axis=0).astype(f32)
        out_ref[:, at] = (gradient * z).astype(bf16)


def gate_kernel(top_ref, bottom_ref, gate_ref, *rest):
    gz_ref = rest[-1]
    half = top_ref.shape[0]
    gz_ref[:half] = (top_ref[...].astype(f32) * gate_ref[:half].astype(f32)).astype(bf16)
    gz_ref[half:] = (bottom_ref[...].astype(f32) * gate_ref[half:].astype(f32)).astype(bf16)


def backward_kernel(taps_ref, own_ref, halo_ref, tot_ref, x_ref, gate_ref, *rest):
    out_ref, gn_ref, inner_ref, scale, acc_ref = rest[-5:]
    step = pl.program_id(0)

    @pl.when(step == 0)
    def _():
        scale[...] = scale_of(tot_ref)
        acc_ref[...] = jnp.zeros_like(acc_ref)

    taps = taps_ref[...].astype(f32)
    masks = band_masks(HEIGHT, taps.shape[1], False)
    for sub in range(own_ref.shape[1] // LANES):
        at = lanes_of(sub)
        signal = jnp.concatenate([own_ref[:, at], halo_ref[:, at]], axis=0)
        gu = filtered_block(taps[groups_of(sub)], signal, masks)
        normed = x_ref[:, at].astype(f32) * scale[...]
        out_ref[:, at] = (gu * normed).astype(bf16)
        gn = gu * gate_ref[:, at].astype(f32)
        gn_ref[:, at] = gn.astype(bf16)
        acc_ref[...] += gn * normed

    @pl.when(step == pl.num_programs(0) - 1)
    def _():
        inner_ref[...] = lane_sums(acc_ref[...])


def input_gradient(gn_ref, x_ref, at, scale, mean):
    normed = x_ref[:, at].astype(f32) * scale[...]
    return (scale[...] * (gn_ref[:, at].astype(f32) - normed * mean[...])).astype(bf16)


def between_kernel(gn_ref, x_ref, tot_ref, inner_ref, z_ref, gate_ref, *rest):
    out_ref, gz_ref, scale, mean = rest[-4:]

    @pl.when(pl.program_id(0) == 0)
    def _():
        scale[...] = scale_of(tot_ref)
        mean[...] = down_rows(inner_ref[0:1, :] / D)

    for sub in range(x_ref.shape[1] // LANES):
        at = lanes_of(sub)
        gradient = input_gradient(gn_ref, x_ref, at, scale, mean).astype(f32)
        gz_ref[:, at] = (gate_ref[:, at].astype(f32) * gradient).astype(bf16)
        out_ref[:, at] = (gradient * z_ref[:, at].astype(f32)).astype(bf16)


def finish_kernel(gn_ref, x_ref, tot_ref, inner_ref, *rest):
    top_ref, bottom_ref, scale, mean = rest[-4:]
    half = top_ref.shape[0]

    @pl.when(pl.program_id(0) == 0)
    def _():
        scale[...] = scale_of(tot_ref)
        mean[...] = down_rows(inner_ref[0:1, :] / D)

    for sub in range(x_ref.shape[1] // LANES):
        at = lanes_of(sub)
        gradient = input_gradient(gn_ref, x_ref, at, scale, mean)
        top_ref[:, at] = gradient[:half]
        bottom_ref[:, at] = gradient[half:]


def fold_kernel(odd_ref, first_ref, second_ref, *rest):
    out_ref = rest[-1]
    half = first_ref.shape[0]
    odd = odd_ref[0]

    @pl.when(odd == 0)
    def _():
        out_ref[:half] = first_ref[...]
        out_ref[half:] = second_ref[...]

    @pl.when(odd != 0)
    def _():
        out_ref[:half] = second_ref[...]
        out_ref[half:] = first_ref[...]


def taps_kernel(seqs, *refs):
    per = 3
    ins, (out_ref, flipped) = refs[: per * seqs], refs[-2:]
    rows = ins[0].shape[0]
    half = rows // 2
    count = LANES // GROUP
    step = pl.program_id(0)

    owner = lax.broadcasted_iota(jnp.int32, (half, LANES), 1) // GROUP
    row = lax.broadcasted_iota(jnp.int32, (half, LANES), 0)
    col = lax.broadcasted_iota(jnp.int32, (half, LANES), 1)
    masks = [(owner == g).astype(bf16) for g in range(count)]
    blocks = ins[0].shape[1] // LANES
    found = []
    for sub in range(blocks):
        at = lanes_of(sub)
        grads = []
        signals = []
        for s in range(seqs):
            gz_ref, own_ref, halo_ref = ins[per * s : per * s + 3]
            grads += [gz_ref[:half, at], gz_ref[half:, at]]
            signal = jnp.concatenate([halo_ref[:, at], own_ref[:, at]], axis=0)
            signals.append(windows(signal, half))
        wide = jnp.concatenate(grads, axis=1)
        left = jnp.concatenate(
            [wide * jnp.concatenate([masks[g]] * len(grads), axis=1) for g in range(count)],
            axis=0,
        )
        products = lax.dot_general(
            left,
            jnp.concatenate(signals, axis=1),
            (((1,), (1,)), ((), ())),
            preferred_element_type=f32,
        )
        slabs = []
        for g in range(count):
            mine = products[g * half : (g + 1) * half]
            wheel = jnp.where(col > row, mine[:, :LANES], mine[:, LANES:])
            slab = wheel[:SUB]
            for a in range(SUB, half, SUB):
                slab = slab + pltpu.roll(wheel[a : a + SUB], LANES - a, 1)
            slabs.append(slab)
        slabs = jnp.concatenate(slabs, axis=0)
        within = lax.rem(lax.broadcasted_iota(jnp.int32, slabs.shape, 0), SUB)
        for bit in (1, 2, 4):
            turned = pltpu.roll(slabs, LANES - bit, 1)
            slabs = jnp.where(within & bit != 0, turned, slabs)
        found.append(jnp.sum(slabs.reshape(count, SUB, LANES), axis=1))
    here = blocks * count
    flipped[pl.ds(pl.multiple_of(step * here, here), here), :] = jnp.concatenate(found, axis=0)

    @pl.when(step == pl.num_programs(0) - 1)
    def _():
        out_ref[...] = lax.dot_general(
            lag_flip(out_ref.shape[0]),
            flipped[...].astype(bf16),
            (((1,), (1,)), ((), ())),
            preferred_element_type=f32,
        )


class Calls:
    def __init__(self, rows, width, taps):
        self.rows, self.width, self.taps = rows, width, taps
        self.block = min(BLOCK, width)
        self.steps = width // self.block
        self.latest = None

    def flat(self, array, s=None, layer=None, rows=None):
        rows = self.rows if rows is None else rows
        lead = tuple(i for i in (layer, s) if i is not None)
        spec = pl.BlockSpec(
            (None,) * len(lead) + (rows, self.block), lambda j, *_: lead + (0, j)
        )
        return array, spec

    def small(self, array=None, s=0):
        return array, pl.BlockSpec((SUB, self.rows), lambda j, *_: (s, 0))

    def filters(self, array, layer):
        count = self.block // GROUP
        return array, pl.BlockSpec((None, count, self.taps), lambda j, *_: (layer, j, 0))

    def square(self):
        return pltpu.VMEM((self.rows, self.rows), f32)

    def call(self, kernel, name, ins, outs, scratch=(), carry=None, prefetch=()):
        operands = [a for a, _ in ins]
        in_specs = [b for _, b in ins]
        aliases = {}
        if self.latest is not None and self.latest is not carry:
            operands.append(self.latest)
            in_specs.append(pl.BlockSpec(memory_space=pl.ANY))
        if carry is not None:
            aliases = {len(prefetch) + len(operands): 0}
            operands.append(carry)
            in_specs.append(pl.BlockSpec(memory_space=pl.ANY))
        results = pl.pallas_call(
            kernel,
            name=name,
            out_shape=[jax.ShapeDtypeStruct(s, d) for s, d, _ in outs],
            grid_spec=pltpu.PrefetchScalarGridSpec(
                num_scalar_prefetch=len(prefetch),
                grid=(self.steps,),
                in_specs=in_specs,
                out_specs=[b for _, _, b in outs],
                scratch_shapes=list(scratch),
            ),
            input_output_aliases=aliases,
            compiler_params=pltpu.CompilerParams(
                dimension_semantics=("arbitrary",), vmem_limit_bytes=VMEM_LIMIT
            ),
            cost_estimate=pl.CostEstimate(
                flops=1, bytes_accessed=1, transcendentals=0
            ),
        )(*prefetch, *operands)
        self.latest = results[-1]
        return results


def shifted(value, steps):
    count = lax.axis_size("ctx")
    first, last = max(0, -steps), min(count, count - steps)
    return lax.ppermute(value, "ctx", [(r, r + steps) for r in range(first, last)])


def over_channels(value):
    if lax.axis_size("ch") == 2:
        return value + lax.ppermute(value, "ch", [(0, 1), (1, 0)])
    return lax.psum(value, "ch")


def owner_routes(count):
    blocks = [[], []]
    for block in range(2 * count):
        folded = block if block < count else 2 * count - 1 - block
        blocks[block % 2].append((folded, block // 2))
    return blocks


def local(activations, grad_in, gate_out, gate_in, filters):
    seqs, rows, width = activations.shape
    taps = filters.shape[2]
    assert rows == taps == LANES
    half = rows // 2
    last = LAYERS - 1
    c = Calls(rows, width, taps)
    one = ((rows, width), bf16, c.flat(None)[1])
    part = ((half, width), bf16, c.flat(None, rows=half)[1])
    vector = ((SUB, rows), f32, c.small()[1])
    whole = (gate_out.shape, bf16)
    routes = owner_routes(lax.axis_size("ctx"))
    odd = lax.rem(lax.axis_index("ctx"), 2)

    def table():
        return [[None] * seqs for _ in range(LAYERS)]

    x, z, u, u_halo, tot = table(), table(), table(), table(), table()
    gz, gz_halo, gn, inner = table(), table(), table(), table()
    done = {"out": None, "in": None, "fold": None}
    found = [None] * LAYERS
    returned = [[None, None] for _ in range(seqs)]
    arrived = [None, None]

    def squares():
        (ssq,) = c.call(
            squares_kernel, "squares",
            [(activations, pl.BlockSpec((seqs, rows, c.block), lambda j: (0, 0, j)))],
            [((seqs * SUB, rows), f32, pl.BlockSpec((seqs * SUB, rows), lambda j: (0, 0)))],
            [pltpu.VMEM((seqs, rows, rows), f32)],
        )
        total = over_channels(ssq)
        for s in range(seqs):
            x[0][s] = c.flat(activations, s)
            tot[0][s] = c.small(total, s)

    def gated_input(layer, s):
        (u[layer][s],) = c.call(
            input_kernel, "input",
            [x[layer][s], tot[layer][s], c.flat(gate_in, s, layer)], [one], [c.square()],
        )
        u_halo[layer][s] = shifted(u[layer][s], 1)

    def arrive():
        held, _ = lax.optimization_barrier((grad_in, c.latest))
        for side in range(2):
            start = jnp.where(odd == side, 0, half)
            piece = lax.dynamic_slice_in_dim(held, start, half, axis=1)
            arrived[side] = lax.ppermute(piece, "ctx", routes[side])

    def arrived_of(s):
        return [c.flat(arrived[side], s, rows=half) for side in range(2)]

    def forward(layer, s):
        z[layer][s], nx, ssq = c.call(
            forward_kernel, "forward",
            [c.filters(filters, layer), c.flat(u[layer][s]), c.flat(u_halo[layer][s]),
             c.flat(gate_out, s, layer)],
            [one, one, vector], [c.square()],
        )
        x[layer + 1][s] = c.flat(nx)
        tot[layer + 1][s] = c.small(over_channels(ssq))

    def last_forward(s):
        (done["out"],) = c.call(
            last_forward_kernel, "last_forward",
            [c.filters(filters, last), c.flat(u[last][s]), c.flat(u_halo[last][s])]
            + arrived_of(s),
            [whole + (c.flat(None, s, last)[1],)], carry=done["out"],
        )

    def first_gate(s):
        (gz[last][s],) = c.call(
            gate_kernel, "gate", arrived_of(s) + [c.flat(gate_out, s, last)], [one]
        )
        gz_halo[last][s] = shifted(gz[last][s], -1)

    def backward(layer, s):
        done["in"], gn[layer][s], found_inner = c.call(
            backward_kernel, "backward",
            [c.filters(filters, layer), c.flat(gz[layer][s]), c.flat(gz_halo[layer][s]),
             tot[layer][s], x[layer][s], c.flat(gate_in, s, layer)],
            [whole + (c.flat(None, s, layer)[1],), one, vector],
            [c.square()] * 2, carry=done["in"],
        )
        inner[layer][s] = c.small(over_channels(found_inner))

    def common(layer, s):
        return [c.flat(gn[layer][s]), x[layer][s], tot[layer][s], inner[layer][s]]

    def between(layer, s):
        done["out"], gz[layer - 1][s] = c.call(
            between_kernel, "between",
            common(layer, s) + [c.flat(z[layer - 1][s]), c.flat(gate_out, s, layer - 1)],
            [whole + (c.flat(None, s, layer - 1)[1],), one],
            [c.square()] * 2, carry=done["out"],
        )
        gz_halo[layer - 1][s] = shifted(gz[layer - 1][s], -1)

    def finish(s):
        halves = c.call(
            finish_kernel, "finish", common(0, s), [part, part], [c.square()] * 2
        )
        for side in range(2):
            back = [(d, r) for r, d in routes[side]]
            returned[s][side] = lax.ppermute(halves[side], "ctx", back)

    def taps_of(layer):
        ins = []
        for s in range(seqs):
            ins += [c.flat(gz[layer][s]), c.flat(u[layer][s]), c.flat(u_halo[layer][s])]
        groups = width // GROUP
        (found[layer],) = c.call(
            functools.partial(taps_kernel, seqs), "taps", ins,
            [((taps, groups), f32, pl.BlockSpec((taps, groups), lambda j: (0, 0)))],
            [pltpu.VMEM((groups, taps), f32)],
        )

    def fold(s):
        (done["fold"],) = c.call(
            fold_kernel, "fold",
            [c.flat(returned[s][side], rows=half) for side in range(2)],
            [(activations.shape, bf16, c.flat(None, s)[1])],
            carry=done["fold"], prefetch=(odd.reshape(1).astype(jnp.int32),),
        )

    squares()
    for s in range(seqs):
        gated_input(0, s)
    arrive()
    for s in range(seqs):
        forward(0, s)
        gated_input(1, s)
    for s in range(seqs):
        first_gate(s)
    for layer in range(1, last):
        for s in range(seqs):
            forward(layer, s)
            gated_input(layer + 1, s)
    for s in range(seqs):
        backward(last, s)
    for s in range(seqs):
        between(last, s)
    for s in range(seqs):
        last_forward(s)
    for layer in reversed(range(1, last)):
        for s in range(seqs):
            backward(layer, s)
            between(layer, s)
        taps_of(layer + 1)
    for s in range(seqs):
        backward(0, s)
        finish(s)
    for layer in reversed(range(min(2, LAYERS))):
        taps_of(layer)

    count = lax.axis_size("ctx")
    mine = lax.all_to_all(jnp.stack(found), "ctx", split_axis=1, concat_axis=1, tiled=True)
    mine = jnp.sum(mine.reshape(LAYERS, count, taps // count, width // GROUP), axis=1)
    grad_filters = jnp.swapaxes(mine, 1, 2)
    for s in range(seqs):
        fold(s)
    return done["fold"], done["out"], done["in"], grad_filters


def solution(mesh):
    return jax.shard_map(
        local,
        mesh=mesh,
        in_specs=(
            P(None, "ctx", "ch"),
            P(None, "ctx", "ch"),
            P(None, None, "ctx", "ch"),
            P(None, None, "ctx", "ch"),
            P(None, "ch", None),
        ),
        out_specs=(
            P(None, "ctx", "ch"),
            P(None, None, "ctx", "ch"),
            P(None, None, "ctx", "ch"),
            P(None, "ch", "ctx"),
        ),
        check_vma=False,
    )
```

profile of v0, /device:TPU:0, one launch (start us, length us, event | category | flops | bytes accessed | tf_op | source)
XLA Modules:
  0.0 323.6 jit_solution(2942694599048588142)
XLA Ops:
  19.7 4.7 %collective-permute-start.3 = (bf16[128,4096]{1,0:T(8,128)(2,1)S(1)}, bf16[128,4096]{1,0:T(8,128)(2,1)S(1)}, u32[]{:S(2)}, u32[]{:S(2)}) collective-permute-start(bf16[128,4096]{1,0:T(8,128)(2,1)S(1)} %input.7.rest_0_.own_ref.refs_4_), channel_id=1, source_target_pairs={{0,2},{2,4},{4,6},{6,8},{8,10},{10,12},{12,14},{14,16},{16,18},{18... | collective-permute-start | bytes 3145736 | tf_op jit(solution)/shard_map/ppermute | solution.py:386
  25.3 7.8 %collective-permute-start.2 = (bf16[2,64,4096]{2,1,0:T(8,128)(2,1)S(1)}, bf16[2,64,4096]{2,1,0:T(8,128)(2,1)S(1)}, u32[]{:S(2)}, u32[]{:S(2)}) collective-permute-start(bf16[2,64,4096]{2,1,0:T(8,128)(2,1)S(1)} %get-tuple-element.94), channel_id=1, source_target_pairs={{2,0},{6,2},{10,4},{14,6},{18,8},{22,10},{26,12},{30,14},{28,16},{... | collective-permute-start | bytes 3145736 | tf_op jit(solution)/shard_map/ppermute | solution.py:451
  33.2 4.4 %forward.4 = (bf16[128,4096]{1,0:T(8,128)(2,1)S(1)}, bf16[128,4096]{1,0:T(8,128)(2,1)S(1)}, f32[8,128]{1,0:T(8,128)S(1)}) custom-call(bf16[3,256,128]{2,1,0:T(8,128)(2,1)S(1)} %copy-done.7, bf16[128,4096]{1,0:T(8,128)(2,1)S(1)} %input.6.rest_0_.own_ref.refs_1_, bf16[128,4096]{1,0:T(8,128)(2,1)S(1)} %collective-permute-done.4.halo_ref.refs_2_, ...), custom_call_target="tpu_custom_call" | custom-call | flops 1 | bytes 1 | tf_op jit(solution)/shard_map/forward/pallas_call | solution.py:360
  42.2 24.2 %collective-permute-start.9 = (bf16[128,4096]{1,0:T(8,128)(2,1)S(1)}, bf16[128,4096]{1,0:T(8,128)(2,1)S(1)}, u32[]{:S(2)}, u32[]{:S(2)}) collective-permute-start(bf16[128,4096]{1,0:T(8,128)(2,1)S(1)} %input.8.rest_0_.own_ref.refs_1_), channel_id=1, source_target_pairs={{0,2},{2,4},{4,6},{6,8},{8,10},{10,12},{12,14},{14,16},{16,18},{18... | collective-permute-start | bytes 3145736 | tf_op jit(solution)/shard_map/ppermute | solution.py:386
  93.2 4.4 %forward.7 = (bf16[128,4096]{1,0:T(8,128)(2,1)S(1)}, bf16[128,4096]{1,0:T(8,128)(2,1)S(1)}, f32[8,128]{1,0:T(8,128)S(1)}) custom-call(bf16[3,256,128]{2,1,0:T(8,128)(2,1)S(1)} %copy-done.7, bf16[128,4096]{1,0:T(8,128)(2,1)S(1)} %input.9.rest_0_.own_ref.refs_4_, bf16[128,4096]{1,0:T(8,128)(2,1)S(1)} %collective-permute-done.8.halo_ref.refs_5_, ...), custom_call_target="tpu_custom_call" | custom-call | flops 1 | bytes 1 | tf_op jit(solution)/shard_map/forward/pallas_call | solution.py:360
  102.1 4.7 %backward.6 = (bf16[3,2,128,4096]{3,2,1,0:T(8,128)(2,1)}, bf16[128,4096]{1,0:T(8,128)(2,1)S(1)}, f32[8,128]{1,0:T(8,128)S(1)}) custom-call(bf16[3,256,128]{2,1,0:T(8,128)(2,1)S(1)} %copy-done.7, bf16[128,4096]{1,0:T(8,128)(2,1)S(1)} %gate.2.rest_0_.own_ref.refs_0_, bf16[128,4096]{1,0:T(8,128)(2,1)S(1)} %collective-permute-done.12.halo_ref, ...), custom_call_target="tpu_custom_call" | custom-call | flops 1 | bytes 1 | tf_op jit(solution)/shard_map/backward/pallas_call | solution.py:360
  108.3 22.7 %collective-permute-start.18 = (bf16[128,4096]{1,0:T(8,128)(2,1)S(1)}, bf16[128,4096]{1,0:T(8,128)(2,1)S(1)}, u32[]{:S(2)}, u32[]{:S(2)}) collective-permute-start(bf16[128,4096]{1,0:T(8,128)(2,1)S(1)} %input.10.rest_0_.own_ref.refs_1_), channel_id=1, source_target_pairs={{0,2},{2,4},{4,6},{6,8},{8,10},{10,12},{12,14},{14,16},{16,18},{18... | collective-permute-start | bytes 3145736 | tf_op jit(solution)/shard_map/ppermute | solution.py:386
  131.0 5.8 %collective-permute-start.17 = (bf16[128,4096]{1,0:T(8,128)(2,1)S(1)}, bf16[128,4096]{1,0:T(8,128)(2,1)S(1)}, u32[]{:S(2)}, u32[]{:S(2)}) collective-permute-start(bf16[128,4096]{1,0:T(8,128)(2,1)S(1)} %input.11.rest_0_.own_ref.refs_4_), channel_id=1, source_target_pairs={{0,2},{2,4},{4,6},{6,8},{8,10},{10,12},{12,14},{14,16},{16,18},{18... | collective-permute-start | bytes 3145736 | tf_op jit(solution)/shard_map/ppermute | solution.py:386
  136.9 4.7 %backward.7 = (bf16[3,2,128,4096]{3,2,1,0:T(8,128)(2,1)}, bf16[128,4096]{1,0:T(8,128)(2,1)S(1)}, f32[8,128]{1,0:T(8,128)S(1)}) custom-call(bf16[3,256,128]{2,1,0:T(8,128)(2,1)S(1)} %copy-done.7, bf16[128,4096]{1,0:T(8,128)(2,1)S(1)} %gate.3.rest_0_.own_ref.refs_3_, ...), custom_call_target="tpu_custom_call", output_to_operand_aliasing={{0}: (7, {})} | custom-call | flops 1 | bytes 1 | tf_op jit(solution)/shard_map/backward/pallas_call | solution.py:360
  153.0 4.7 %last_forward.2.rest_0_ = bf16[3,2,128,4096]{3,2,1,0:T(8,128)(2,1)} custom-call(bf16[3,256,128]{2,1,0:T(8,128)(2,1)S(1)} %copy-done.7, bf16[128,4096]{1,0:T(8,128)(2,1)S(1)} %input.10.rest_0_.own_ref.refs_1_, bf16[128,4096]{1,0:T(8,128)(2,1)S(1)} %collective-permute-done.18.halo_ref.refs_2_, ...), custom_call_target="tpu_custom_call", output_to_operand_aliasing={{}: (6, {})} | custom-call | flops 1 | bytes 1 | tf_op jit(solution)/shard_map/last_forward/pallas_call | solution.py:360
  157.7 4.7 %last_forward.3.rest_0_.rest_1_ = bf16[3,2,128,4096]{3,2,1,0:T(8,128)(2,1)} custom-call(bf16[3,256,128]{2,1,0:T(8,128)(2,1)S(1)} %copy-done.7, bf16[128,4096]{1,0:T(8,128)(2,1)S(1)} %input.11.rest_0_.own_ref.refs_4_, bf16[128,4096]{1,0:T(8,128)(2,1)S(1)} %collective-permute-done.17.halo_ref.refs_5_, ...), custom_call_target="tpu_custom_call", output_to_operand_aliasing={{}: (5, {})} | custom-call | flops 1 | bytes 1 | tf_op jit(solution)/shard_map/last_forward/pallas_call | solution.py:360
  165.1 4.7 %backward.8 = (bf16[3,2,128,4096]{3,2,1,0:T(8,128)(2,1)}, bf16[128,4096]{1,0:T(8,128)(2,1)S(1)}, f32[8,128]{1,0:T(8,128)S(1)}) custom-call(bf16[3,256,128]{2,1,0:T(8,128)(2,1)S(1)} %copy-done.7, bf16[128,4096]{1,0:T(8,128)(2,1)S(1)} %get-tuple-element.63.rest_0_.own_ref.refs_0_, ...), custom_call_target="tpu_custom_call", output_to_operand_aliasing={{0}: (7, {})} | custom-call | flops 1 | bytes 1 | tf_op jit(solution)/shard_map/backward/pallas_call | solution.py:360
  177.2 4.7 %backward.9 = (bf16[3,2,128,4096]{3,2,1,0:T(8,128)(2,1)}, bf16[128,4096]{1,0:T(8,128)(2,1)S(1)}, f32[8,128]{1,0:T(8,128)S(1)}) custom-call(bf16[3,256,128]{2,1,0:T(8,128)(2,1)S(1)} %copy-done.7, bf16[128,4096]{1,0:T(8,128)(2,1)S(1)} %get-tuple-element.65.rest_0_.own_ref.refs_3_, ...), custom_call_target="tpu_custom_call", output_to_operand_aliasing={{0}: (7, {})} | custom-call | flops 1 | bytes 1 | tf_op jit(solution)/shard_map/backward/pallas_call | solution.py:360
  189.5 7.0 %taps.3.rest_0_ = f32[128,256]{1,0:T(8,128)S(1)} custom-call(bf16[128,4096]{1,0:T(8,128)(2,1)S(1)} %gate.2.rest_0_.own_ref.refs_0_, bf16[128,4096]{1,0:T(8,128)(2,1)S(1)} %input.10.rest_0_.own_ref.refs_1_, bf16[128,4096]{1,0:T(8,128)(2,1)S(1)} %collective-permute-done.18.halo_ref.refs_2_, bf16[128,4096]{1,0:T(8,128)(2,1)S(1)} %gate.3.rest_0_.own_ref.refs_3_, ...), custom_call_target="tpu_custom_call" | custom-call | flops 1 | bytes 1 | tf_op jit(solution)/shard_map/taps/pallas_call | solution.py:360
  196.5 4.9 %collective-permute-done.22.halo_ref = bf16[128,4096]{1,0:T(8,128)(2,1)S(1)} collective-permute-done((bf16[128,4096]{1,0:T(8,128)(2,1)S(1)}, bf16[128,4096]{1,0:T(8,128)(2,1)S(1)}, u32[]{:S(2)}, u32[]{:S(2)}) %collective-permute-start.22) | collective-permute-done | bytes 1048608 | tf_op jit(solution)/shard_map/ppermute | solution.py:386
  201.4 4.7 %backward.10 = (bf16[3,2,128,4096]{3,2,1,0:T(8,128)(2,1)}, bf16[128,4096]{1,0:T(8,128)(2,1)S(1)}, f32[8,128]{1,0:T(8,128)S(1)}) custom-call(bf16[3,256,128]{2,1,0:T(8,128)(2,1)S(1)} %copy-done.7, bf16[128,4096]{1,0:T(8,128)(2,1)S(1)} %get-tuple-element.71.rest_0_.own_ref.refs_0_, ...), custom_call_target="tpu_custom_call", output_to_operand_aliasing={{0}: (7, {})} | custom-call | flops 1 | bytes 1 | tf_op jit(solution)/shard_map/backward/pallas_call | solution.py:360
  213.2 4.7 %backward.11 = (bf16[3,2,128,4096]{3,2,1,0:T(8,128)(2,1)}, bf16[128,4096]{1,0:T(8,128)(2,1)S(1)}, f32[8,128]{1,0:T(8,128)S(1)}) custom-call(bf16[3,256,128]{2,1,0:T(8,128)(2,1)S(1)} %copy-done.7, bf16[128,4096]{1,0:T(8,128)(2,1)S(1)} %get-tuple-element.77.refs_6_.own_ref.refs_3_, ...), custom_call_target="tpu_custom_call", output_to_operand_aliasing={{0}: (7, {})} | custom-call | flops 1 | bytes 1 | tf_op jit(solution)/shard_map/backward/pallas_call | solution.py:360
  222.4 7.0 %taps.4.refs_6_ = f32[128,256]{1,0:T(8,128)S(1)} custom-call(bf16[128,4096]{1,0:T(8,128)(2,1)S(1)} %get-tuple-element.63.rest_0_.own_ref.refs_0_, bf16[128,4096]{1,0:T(8,128)(2,1)S(1)} %input.8.rest_0_.own_ref.refs_1_, bf16[128,4096]{1,0:T(8,128)(2,1)S(1)} %copy-done.11, bf16[128,4096]{1,0:T(8,128)(2,1)S(1)} %get-tuple-element.65.rest_0_.own_ref.refs_3_, ...), custom_call_target="tpu_custom_call" | custom-call | flops 1 | bytes 1 | tf_op jit(solution)/shard_map/taps/pallas_call | solution.py:360
  229.4 7.0 %taps.5.rest_0_ = f32[128,256]{1,0:T(8,128)S(1)} custom-call(bf16[128,4096]{1,0:T(8,128)(2,1)S(1)} %get-tuple-element.71.rest_0_.own_ref.refs_0_, bf16[128,4096]{1,0:T(8,128)(2,1)S(1)} %input.6.rest_0_.own_ref.refs_1_, bf16[128,4096]{1,0:T(8,128)(2,1)S(1)} %collective-permute-done.4.halo_ref.refs_2_, ...), custom_call_target="tpu_custom_call" | custom-call | flops 1 | bytes 1 | tf_op jit(solution)/shard_map/taps/pallas_call | solution.py:360
  237.5 24.7 %all-to-all-start = ((f32[3,128,256]{2,0,1:T(4,128)}), f32[3,128,256]{2,0,1:T(4,128)S(1)}, u32[]{:S(2)}, u32[]{:S(2)}) async-start(f32[3,128,256]{2,0,1:T(4,128)} %copy.21), calls=%async_computation | async-start | bytes 1048576 | tf_op jit(solution)/shard_map/all_to_all | solution.py:560
  263.0 5.2 %collective-permute-start.28 = (bf16[64,4096]{1,0:T(8,128)(2,1)S(1)}, bf16[64,4096]{1,0:T(8,128)(2,1)S(1)}, u32[]{:S(2)}, u32[]{:S(2)}) collective-permute-start(bf16[64,4096]{1,0:T(8,128)(2,1)S(1)} %get-tuple-element.81.rest_0_), channel_id=1, source_target_pairs={{0,2},{2,6},{4,10},{6,14},{8,18},{10,22},{12,26},{14,30},{16,28},{... | collective-permute-start | bytes 1572872 | tf_op jit(solution)/shard_map/ppermute | solution.py:508
  269.9 5.7 %collective-permute-start.26 = (bf16[64,4096]{1,0:T(8,128)(2,1)S(1)}, bf16[64,4096]{1,0:T(8,128)(2,1)S(1)}, u32[]{:S(2)}, u32[]{:S(2)}) collective-permute-start(bf16[64,4096]{1,0:T(8,128)(2,1)S(1)} %get-tuple-element.86.refs_6_), channel_id=1, source_target_pairs={{0,2},{2,6},{4,10},{6,14},{8,18},{10,22},{12,26},{14,30},{16,28},{... | collective-permute-start | bytes 1572872 | tf_op jit(solution)/shard_map/ppermute | solution.py:508
  275.5 23.2 %collective-permute-done.28.second_ref = bf16[64,4096]{1,0:T(8,128)(2,1)S(1)} collective-permute-done((bf16[64,4096]{1,0:T(8,128)(2,1)S(1)}, bf16[64,4096]{1,0:T(8,128)(2,1)S(1)}, u32[]{:S(2)}, u32[]{:S(2)}) %collective-permute-start.28) | collective-permute-done | bytes 524320 | tf_op jit(solution)/shard_map/ppermute | solution.py:508
  300.4 20.8 %collective-permute-done.26.second_ref = bf16[64,4096]{1,0:T(8,128)(2,1)S(1)} collective-permute-done((bf16[64,4096]{1,0:T(8,128)(2,1)S(1)}, bf16[64,4096]{1,0:T(8,128)(2,1)S(1)}, u32[]{:S(2)}, u32[]{:S(2)}) %collective-permute-start.26) | collective-permute-done | bytes 524320 | tf_op jit(solution)/shard_map/ppermute | solution.py:508
  (134 shorter events, 105.3 us)
Async XLA Ops:
  3.0 4.6 %collective-permute-start = (f32[16,128]{1,0:T(8,128)S(1)}, f32[16,128]{1,0:T(8,128)S(1)}, u32[]{:S(2)}, u32[]{:S(2)}) collective-permute-start(f32[16,128]{1,0:T(8,128)S(1)} %squares.1.rest_0_), channel_id=1, source_target_pairs={{0,1},{1,0},{2,3},{3,2},{4,5},{5,4},{6,7},{7,6},{8,9},{9,8},{10,11... | collective-permute-start | bytes 24584 | tf_op jit(solution)/shard_map/ppermute | solution.py:391
  18.0 15.1 %collective-permute-start.4 = (bf16[128,4096]{1,0:T(8,128)(2,1)S(1)}, bf16[128,4096]{1,0:T(8,128)(2,1)S(1)}, u32[]{:S(2)}, u32[]{:S(2)}) collective-permute-start(bf16[128,4096]{1,0:T(8,128)(2,1)S(1)} %input.6.rest_0_.own_ref.refs_1_), channel_id=1, source_target_pairs={{0,2},{2,4},{4,6},{6,8},{8,10},{10,12},{12,14},{14,16},{16,18},{18... | collective-permute-start | bytes 3145736 | tf_op jit(solution)/shard_map/ppermute | solution.py:386
  19.7 46.7 %collective-permute-start.3 = (bf16[128,4096]{1,0:T(8,128)(2,1)S(1)}, bf16[128,4096]{1,0:T(8,128)(2,1)S(1)}, u32[]{:S(2)}, u32[]{:S(2)}) collective-permute-start(bf16[128,4096]{1,0:T(8,128)(2,1)S(1)} %input.7.rest_0_.own_ref.refs_4_), channel_id=1, source_target_pairs={{0,2},{2,4},{4,6},{6,8},{8,10},{10,12},{12,14},{14,16},{16,18},{18... | collective-permute-start | bytes 3145736 | tf_op jit(solution)/shard_map/ppermute | solution.py:386
  24.6 56.0 %collective-permute-start.1 = (bf16[2,64,4096]{2,1,0:T(8,128)(2,1)S(1)}, bf16[2,64,4096]{2,1,0:T(8,128)(2,1)S(1)}, u32[]{:S(2)}, u32[]{:S(2)}) collective-permute-start(bf16[2,64,4096]{2,1,0:T(8,128)(2,1)S(1)} %get-tuple-element.95), channel_id=1, source_target_pairs={{0,0},{4,2},{8,4},{12,6},{16,8},{20,10},{24,12},{28,14},{30,16},{2... | collective-permute-start | bytes 3145736 | tf_op jit(solution)/shard_map/ppermute | solution.py:451
  25.3 55.2 %collective-permute-start.2 = (bf16[2,64,4096]{2,1,0:T(8,128)(2,1)S(1)}, bf16[2,64,4096]{2,1,0:T(8,128)(2,1)S(1)}, u32[]{:S(2)}, u32[]{:S(2)}) collective-permute-start(bf16[2,64,4096]{2,1,0:T(8,128)(2,1)S(1)} %get-tuple-element.94), channel_id=1, source_target_pairs={{2,0},{6,2},{10,4},{14,6},{18,8},{22,10},{26,12},{30,14},{28,16},{... | collective-permute-start | bytes 3145736 | tf_op jit(solution)/shard_map/ppermute | solution.py:451
  37.7 3.7 %collective-permute-start.5 = (f32[8,128]{1,0:T(8,128)S(1)}, f32[8,128]{1,0:T(8,128)S(1)}, u32[]{:S(2)}, u32[]{:S(2)}) collective-permute-start(f32[8,128]{1,0:T(8,128)S(1)} %get-tuple-element.49.rest_0_), channel_id=1, source_target_pairs={{0,1},{1,0},{2,3},{3,2},{4,5},{5,4},{6,7},{7,6},{8,9},{9,8},{10,11... | collective-permute-start | bytes 12296 | tf_op jit(solution)/shard_map/ppermute | solution.py:391
  42.2 42.1 %collective-permute-start.9 = (bf16[128,4096]{1,0:T(8,128)(2,1)S(1)}, bf16[128,4096]{1,0:T(8,128)(2,1)S(1)}, u32[]{:S(2)}, u32[]{:S(2)}) collective-permute-start(bf16[128,4096]{1,0:T(8,128)(2,1)S(1)} %input.8.rest_0_.own_ref.refs_1_), channel_id=1, source_target_pairs={{0,2},{2,4},{4,6},{6,8},{8,10},{10,12},{12,14},{14,16},{16,18},{18... | collective-permute-start | bytes 3145736 | tf_op jit(solution)/shard_map/ppermute | solution.py:386
  76.1 17.1 %collective-permute-start.8 = (bf16[128,4096]{1,0:T(8,128)(2,1)S(1)}, bf16[128,4096]{1,0:T(8,128)(2,1)S(1)}, u32[]{:S(2)}, u32[]{:S(2)}) collective-permute-start(bf16[128,4096]{1,0:T(8,128)(2,1)S(1)} %input.9.rest_0_.own_ref.refs_4_), channel_id=1, source_target_pairs={{0,2},{2,4},{4,6},{6,8},{8,10},{10,12},{12,14},{14,16},{16,18},{18... | collective-permute-start | bytes 3145736 | tf_op jit(solution)/shard_map/ppermute | solution.py:386
  81.1 21.0 %collective-permute-start.12 = (bf16[128,4096]{1,0:T(8,128)(2,1)S(1)}, bf16[128,4096]{1,0:T(8,128)(2,1)S(1)}, u32[]{:S(2)}, u32[]{:S(2)}) collective-permute-start(bf16[128,4096]{1,0:T(8,128)(2,1)S(1)} %gate.2.rest_0_.own_ref.refs_0_), channel_id=1, source_target_pairs={{2,0},{4,2},{6,4},{8,6},{10,8},{12,10},{14,12},{16,14},{18,16},{20... | collective-permute-start | bytes 3145736 | tf_op jit(solution)/shard_map/ppermute | solution.py:386
  83.0 53.9 %collective-permute-start.7 = (bf16[128,4096]{1,0:T(8,128)(2,1)S(1)}, bf16[128,4096]{1,0:T(8,128)(2,1)S(1)}, u32[]{:S(2)}, u32[]{:S(2)}) collective-permute-start(bf16[128,4096]{1,0:T(8,128)(2,1)S(1)} %gate.3.rest_0_.own_ref.refs_3_), channel_id=1, source_target_pairs={{2,0},{4,2},{6,4},{8,6},{10,8},{12,10},{14,12},{16,14},{18,16},{20... | collective-permute-start | bytes 3145736 | tf_op jit(solution)/shard_map/ppermute | solution.py:386
  88.7 3.7 %collective-permute-start.10 = (f32[8,128]{1,0:T(8,128)S(1)}, f32[8,128]{1,0:T(8,128)S(1)}, u32[]{:S(2)}, u32[]{:S(2)}) collective-permute-start(f32[8,128]{1,0:T(8,128)S(1)} %get-tuple-element.53.rest_0_), channel_id=1, source_target_pairs={{0,1},{1,0},{2,3},{3,2},{4,5},{5,4},{6,7},{7,6},{8,9},{9,8},{10,11... | collective-permute-start | bytes 12296 | tf_op jit(solution)/shard_map/ppermute | solution.py:391
  97.6 3.7 %collective-permute-start.11 = (f32[8,128]{1,0:T(8,128)S(1)}, f32[8,128]{1,0:T(8,128)S(1)}, u32[]{:S(2)}, u32[]{:S(2)}) collective-permute-start(f32[8,128]{1,0:T(8,128)S(1)} %get-tuple-element.54.rest_0_), channel_id=1, source_target_pairs={{0,1},{1,0},{2,3},{3,2},{4,5},{5,4},{6,7},{7,6},{8,9},{9,8},{10,11... | collective-permute-start | bytes 12296 | tf_op jit(solution)/shard_map/ppermute | solution.py:391
  106.8 34.7 %collective-permute-start.14 = (f32[8,128]{1,0:T(8,128)S(1)}, f32[8,128]{1,0:T(8,128)S(1)}, u32[]{:S(2)}, u32[]{:S(2)}) collective-permute-start(f32[8,128]{1,0:T(8,128)S(1)} %get-tuple-element.56.rest_0_), channel_id=1, source_target_pairs={{0,1},{1,0},{2,3},{3,2},{4,5},{5,4},{6,7},{7,6},{8,9},{9,8},{10,11... | collective-permute-start | bytes 12296 | tf_op jit(solution)/shard_map/ppermute | solution.py:391
  108.3 44.7 %collective-permute-start.18 = (bf16[128,4096]{1,0:T(8,128)(2,1)S(1)}, bf16[128,4096]{1,0:T(8,128)(2,1)S(1)}, u32[]{:S(2)}, u32[]{:S(2)}) collective-permute-start(bf16[128,4096]{1,0:T(8,128)(2,1)S(1)} %input.10.rest_0_.own_ref.refs_1_), channel_id=1, source_target_pairs={{0,2},{2,4},{4,6},{6,8},{8,10},{10,12},{12,14},{14,16},{16,18},{18... | collective-permute-start | bytes 3145736 | tf_op jit(solution)/shard_map/ppermute | solution.py:386
  131.0 26.6 %collective-permute-start.17 = (bf16[128,4096]{1,0:T(8,128)(2,1)S(1)}, bf16[128,4096]{1,0:T(8,128)(2,1)S(1)}, u32[]{:S(2)}, u32[]{:S(2)}) collective-permute-start(bf16[128,4096]{1,0:T(8,128)(2,1)S(1)} %input.11.rest_0_.own_ref.refs_4_), channel_id=1, source_target_pairs={{0,2},{2,4},{4,6},{6,8},{8,10},{10,12},{12,14},{14,16},{16,18},{18... | collective-permute-start | bytes 3145736 | tf_op jit(solution)/shard_map/ppermute | solution.py:386
  144.1 18.3 %collective-permute-start.16 = (bf16[128,4096]{1,0:T(8,128)(2,1)S(1)}, bf16[128,4096]{1,0:T(8,128)(2,1)S(1)}, u32[]{:S(2)}, u32[]{:S(2)}) collective-permute-start(bf16[128,4096]{1,0:T(8,128)(2,1)S(1)} %get-tuple-element.63.rest_0_.own_ref.refs_0_), channel_id=1, source_target_pairs={{2,0},{4,2},{6,4},{8,6},{10,8},{12,10},{14,12},{16,14},{18,16},{20... | collective-permute-start | bytes 3145736 | tf_op jit(solution)/shard_map/ppermute | solution.py:386
  151.5 25.7 %collective-permute-start.15 = (bf16[128,4096]{1,0:T(8,128)(2,1)S(1)}, bf16[128,4096]{1,0:T(8,128)(2,1)S(1)}, u32[]{:S(2)}, u32[]{:S(2)}) collective-permute-start(bf16[128,4096]{1,0:T(8,128)(2,1)S(1)} %get-tuple-element.65.rest_0_.own_ref.refs_3_), channel_id=1, source_target_pairs={{2,0},{4,2},{6,4},{8,6},{10,8},{12,10},{14,12},{16,14},{18,16},{20... | collective-permute-start | bytes 3145736 | tf_op jit(solution)/shard_map/ppermute | solution.py:386
  175.9 25.5 %collective-permute-start.22 = (bf16[128,4096]{1,0:T(8,128)(2,1)S(1)}, bf16[128,4096]{1,0:T(8,128)(2,1)S(1)}, u32[]{:S(2)}, u32[]{:S(2)}) collective-permute-start(bf16[128,4096]{1,0:T(8,128)(2,1)S(1)} %get-tuple-element.71.rest_0_.own_ref.refs_0_), channel_id=1, source_target_pairs={{2,0},{4,2},{6,4},{8,6},{10,8},{12,10},{14,12},{16,14},{18,16},{20... | collective-permute-start | bytes 3145736 | tf_op jit(solution)/shard_map/ppermute | solution.py:386
  188.1 25.1 %collective-permute-start.21 = (bf16[128,4096]{1,0:T(8,128)(2,1)S(1)}, bf16[128,4096]{1,0:T(8,128)(2,1)S(1)}, u32[]{:S(2)}, u32[]{:S(2)}) collective-permute-start(bf16[128,4096]{1,0:T(8,128)(2,1)S(1)} %get-tuple-element.77.refs_6_.own_ref.refs_3_), channel_id=1, source_target_pairs={{2,0},{4,2},{6,4},{8,6},{10,8},{12,10},{14,12},{16,14},{18,16},{20... | collective-permute-start | bytes 3145736 | tf_op jit(solution)/shard_map/ppermute | solution.py:386
  237.5 85.3 %all-to-all-start = ((f32[3,128,256]{2,0,1:T(4,128)}), f32[3,128,256]{2,0,1:T(4,128)S(1)}, u32[]{:S(2)}, u32[]{:S(2)}) async-start(f32[3,128,256]{2,0,1:T(4,128)} %copy.21), calls=%async_computation | async-start | bytes 1048576 | tf_op jit(solution)/shard_map/all_to_all | solution.py:560
  262.3 13.2 %collective-permute-start.27 = (bf16[64,4096]{1,0:T(8,128)(2,1)S(1)}, bf16[64,4096]{1,0:T(8,128)(2,1)S(1)}, u32[]{:S(2)}, u32[]{:S(2)}) collective-permute-start(bf16[64,4096]{1,0:T(8,128)(2,1)S(1)} %get-tuple-element.87), channel_id=1, source_target_pairs={{0,0},{2,4},{4,8},{6,12},{8,16},{10,20},{12,24},{14,28},{16,30},{1... | collective-permute-start | bytes 1572872 | tf_op jit(solution)/shard_map/ppermute | solution.py:508
  263.0 35.8 %collective-permute-start.28 = (bf16[64,4096]{1,0:T(8,128)(2,1)S(1)}, bf16[64,4096]{1,0:T(8,128)(2,1)S(1)}, u32[]{:S(2)}, u32[]{:S(2)}) collective-permute-start(bf16[64,4096]{1,0:T(8,128)(2,1)S(1)} %get-tuple-element.81.rest_0_), channel_id=1, source_target_pairs={{0,2},{2,6},{4,10},{6,14},{8,18},{10,22},{12,26},{14,30},{16,28},{... | collective-permute-start | bytes 1572872 | tf_op jit(solution)/shard_map/ppermute | solution.py:508
  268.2 32.2 %collective-permute-start.25 = (bf16[64,4096]{1,0:T(8,128)(2,1)}, bf16[64,4096]{1,0:T(8,128)(2,1)S(1)}, u32[]{:S(2)}, u32[]{:S(2)}) collective-permute-start(bf16[64,4096]{1,0:T(8,128)(2,1)} %copy-done.18), channel_id=1, source_target_pairs={{0,0},{2,4},{4,8},{6,12},{8,16},{10,20},{12,24},{14,28},{16,30},{1... | collective-permute-start | bytes 1572872 | tf_op jit(solution)/shard_map/ppermute | solution.py:508
  269.9 51.4 %collective-permute-start.26 = (bf16[64,4096]{1,0:T(8,128)(2,1)S(1)}, bf16[64,4096]{1,0:T(8,128)(2,1)S(1)}, u32[]{:S(2)}, u32[]{:S(2)}) collective-permute-start(bf16[64,4096]{1,0:T(8,128)(2,1)S(1)} %get-tuple-element.86.refs_6_), channel_id=1, source_target_pairs={{0,2},{2,6},{4,10},{6,14},{8,18},{10,22},{12,26},{14,30},{16,28},{... | collective-permute-start | bytes 1572872 | tf_op jit(solution)/shard_map/ppermute | solution.py:508
  (30 other events, 256.6 us)
where the time goes:
time: 324 us
  starting transfers between devices  131 us (40%)
  Pallas kernels  97.7 us (30%)
  waiting for transfers between devices  76.9 us (24%)
  local copies, waits for them, and re-layouts  16.1 us (5%)
    pallas_call x32, Pallas kernels, call(): pl.pallas_call(kernel, name=name, out_shape=[jax.ShapeDtypeStruct(s, d) f...  97.7 us
    ppermute x12, starting transfers between devices, shifted(): lax.ppermute(value, 'ctx', [(r, r + steps) for r in range(first, last)])  71.4 us
    ppermute x4, waiting for transfers between devices, finish(): returned[s][side] = lax.ppermute(halves[side], 'ctx', back)  44.1 us
    ppermute x11, waiting for transfers between devices, over_channels(): return value + lax.ppermute(value, 'ch', [(0, 1), (1, 0)])  25.4 us
    all_to_all x1, starting transfers between devices, local(): lax.all_to_all(jnp.stack(found), 'ctx', split_axis=1, concat_axis=1, tile...  24.7 us
    unnamed x49, local copies, waits for them, and re-layouts  14.8 us
    ppermute x11, starting transfers between devices, over_channels(): return value + lax.ppermute(value, 'ch', [(0, 1), (1, 0)])  13.5 us
    ppermute x4, starting transfers between devices, finish(): returned[s][side] = lax.ppermute(halves[side], 'ctx', back)  13.2 us
  transfers between devices with their start and end apart: 30, of which 14 were waited for; matrix products, arithmetic and copies ran while one was open for 0% of the time, Pallas kernels for 23%

commit v1 on v0

--- a/solution.py
+++ b/solution.py
@@ -15,7 +15,8 @@
 SUB = 8
 BLOCK = 1024
 HEIGHT = 32
-VMEM_LIMIT = 20 * 1024 * 1024
+VMEM_LIMIT = 28 * 1024 * 1024
+VMEM_MOST = 60 * 1024 * 1024
 
 f32 = jnp.float32
 bf16 = jnp.bfloat16
@@ -321,6 +322,12 @@
         )
 
 
+def pack_kernel(*refs):
+    out_ref = refs[-1]
+    for layer in range(LAYERS):
+        out_ref[layer] = refs[layer][...]
+
+
 class Calls:
     def __init__(self, rows, width, taps):
         self.rows, self.width, self.taps = rows, width, taps
@@ -346,7 +353,7 @@
     def square(self):
         return pltpu.VMEM((self.rows, self.rows), f32)
 
-    def call(self, kernel, name, ins, outs, scratch=(), carry=None, prefetch=()):
+    def call(self, kernel, name, ins, outs, scratch=(), carry=None, prefetch=(), vmem=VMEM_LIMIT):
         operands = [a for a, _ in ins]
         in_specs = [b for _, b in ins]
         aliases = {}
@@ -370,7 +377,7 @@
             ),
             input_output_aliases=aliases,
             compiler_params=pltpu.CompilerParams(
-                dimension_semantics=("arbitrary",), vmem_limit_bytes=VMEM_LIMIT
+                dimension_semantics=("arbitrary",), vmem_limit_bytes=vmem
             ),
             cost_estimate=pl.CostEstimate(
                 flops=1, bytes_accessed=1, transcendentals=0
@@ -429,7 +436,7 @@
             squares_kernel, "squares",
             [(activations, pl.BlockSpec((seqs, rows, c.block), lambda j: (0, 0, j)))],
             [((seqs * SUB, rows), f32, pl.BlockSpec((seqs * SUB, rows), lambda j: (0, 0)))],
-            [pltpu.VMEM((seqs, rows, rows), f32)],
+            [pltpu.VMEM((seqs, rows, rows), f32)], vmem=VMEM_MOST,
         )
         total = over_channels(ssq)
         for s in range(seqs):
@@ -440,14 +447,14 @@
         (u[layer][s],) = c.call(
             input_kernel, "input",
             [x[layer][s], tot[layer][s], c.flat(gate_in, s, layer)], [one], [c.square()],
+            vmem=VMEM_LIMIT if layer else VMEM_MOST,
         )
         u_halo[layer][s] = shifted(u[layer][s], 1)
 
     def arrive():
-        held, _ = lax.optimization_barrier((grad_in, c.latest))
         for side in range(2):
             start = jnp.where(odd == side, 0, half)
-            piece = lax.dynamic_slice_in_dim(held, start, half, axis=1)
+            piece = lax.dynamic_slice_in_dim(grad_in, start, half, axis=1)
             arrived[side] = lax.ppermute(piece, "ctx", routes[side])
 
     def arrived_of(s):
@@ -526,10 +533,22 @@
             carry=done["fold"], prefetch=(odd.reshape(1).astype(jnp.int32),),
         )
 
+    def pack():
+        groups = width // GROUP
+        shape = (LAYERS, taps, groups)
+        spec = pl.BlockSpec((taps, groups), lambda: (0, 0))
+        return pl.pallas_call(
+            pack_kernel,
+            name="pack",
+            out_shape=jax.ShapeDtypeStruct(shape, f32),
+            in_specs=[spec] * LAYERS + [pl.BlockSpec(memory_space=pl.ANY)],
+            out_specs=pl.BlockSpec(shape, lambda: (0, 0, 0)),
+        )(*found, returned[0][0])
+
+    arrive()
     squares()
     for s in range(seqs):
         gated_input(0, s)
-    arrive()
     for s in range(seqs):
         forward(0, s)
         gated_input(1, s)
@@ -541,7 +560,6 @@
             gated_input(layer + 1, s)
     for s in range(seqs):
         backward(last, s)
-    for s in range(seqs):
         between(last, s)
     for s in range(seqs):
         last_forward(s)
@@ -549,15 +567,14 @@
         for s in range(seqs):
             backward(layer, s)
             between(layer, s)
-        taps_of(layer + 1)
+    for layer in reversed(range(LAYERS)):
+        taps_of(layer)
     for s in range(seqs):
         backward(0, s)
         finish(s)
-    for layer in reversed(range(min(2, LAYERS))):
-        taps_of(layer)
 
     count = lax.axis_size("ctx")
-    mine = lax.all_to_all(jnp.stack(found), "ctx", split_axis=1, concat_axis=1, tiled=True)
+    mine = lax.all_to_all(pack(), "ctx", split_axis=1, concat_axis=1, tiled=True)
     mine = jnp.sum(mine.reshape(LAYERS, count, taps // count, width // GROUP), axis=1)
     grad_filters = jnp.swapaxes(mine, 1, 2)
     for s in range(seqs):

time: 324 us -> 325 us (level)
  waiting for transfers between devices: 76.9 us -> 52.2 us
  Pallas kernels: 97.7 us -> 112 us
  starting transfers between devices: 131 us -> 142 us
    ppermute x4, waiting for transfers between devices: 44.1 us -> 29.1 us  [finish(): returned[s][side] = lax.ppermute(halves[side], 'ctx', back)]
    all_to_all x1, starting transfers between devices: 24.7 us -> 38.3 us  [local(): lax.all_to_all(pack(), 'ctx', split_axis=1, concat_axis=1, tiled=True)]
    pallas_call x32, Pallas kernels: 97.7 us -> 111 us  [call(): pl.pallas_call(kernel, name=name, out_shape=[jax.ShapeDtypeStruct(s, d) f...]
    ppermute x12, waiting for transfers between devices: 7.49 us -> 0.03 us  [shifted(): lax.ppermute(value, 'ctx', [(r, r + steps) for r in range(first, last)])]
    ppermute x4, starting transfers between devices: 13.2 us -> 8.73 us  [finish(): returned[s][side] = lax.ppermute(halves[side], 'ctx', back)]
    unnamed x49 -> x85, local copies, waits for them, and re-layouts: 14.8 us -> 11.1 us
  transfers between devices with their start and end apart: 30 -> 30, of which waited for: 14 -> 12; matrix products, arithmetic and copies ran while one was open for 0% -> 1% of each run, Pallas kernels for 23% -> 31%
where the time goes in v1:
time: 325 us; the launch traced here: 324 us
  starting transfers between devices  142 us (44%)
  Pallas kernels  112 us (34%)
  waiting for transfers between devices  52.2 us (16%)
  local copies, waits for them, and re-layouts  13.3 us (4%)
    pallas_call x32, Pallas kernels, call(): pl.pallas_call(kernel, name=name, out_shape=[jax.ShapeDtypeStruct(s, d) f...  111 us
    ppermute x12, starting transfers between devices, shifted(): lax.ppermute(value, 'ctx', [(r, r + steps) for r in range(first, last)])  72.4 us
    all_to_all x1, starting transfers between devices, local(): lax.all_to_all(pack(), 'ctx', split_axis=1, concat_axis=1, tiled=True)  38.3 us
    ppermute x4, waiting for transfers between devices, finish(): returned[s][side] = lax.ppermute(halves[side], 'ctx', back)  29.1 us
    ppermute x11, waiting for transfers between devices, over_channels(): return value + lax.ppermute(value, 'ch', [(0, 1), (1, 0)])  23.1 us
    ppermute x11, starting transfers between devices, over_channels(): return value + lax.ppermute(value, 'ch', [(0, 1), (1, 0)])  13.9 us
    unnamed x85, local copies, waits for them, and re-layouts  11.1 us
    ppermute x4, starting transfers between devices, finish(): returned[s][side] = lax.ppermute(halves[side], 'ctx', back)  8.73 us
  transfers between devices with their start and end apart: 30, of which 12 were waited for; matrix products, arithmetic and copies ran while one was open for 1% of the time, Pallas kernels for 31%

profile of v1, /device:TPU:0, one launch (start us, length us, event | category | flops | bytes accessed | tf_op | source)
XLA Modules:
  0.0 323.8 jit_solution(11293740033624283624)
XLA Ops:
  19.4 4.7 %collective-permute-start.3 = (bf16[128,4096]{1,0:T(8,128)(2,1)}, bf16[128,4096]{1,0:T(8,128)(2,1)S(1)}, u32[]{:S(2)}, u32[]{:S(2)}) collective-permute-start(bf16[128,4096]{1,0:T(8,128)(2,1)} %input.7.rest_0_.own_ref.refs_4_), channel_id=1, source_target_pairs={{0,2},{2,4},{4,6},{6,8},{8,10},{10,12},{12,14},{14,16},{16,18},{18... | collective-permute-start | bytes 3145736 | tf_op jit(solution)/shard_map/ppermute | solution.py:393
  25.0 7.8 %collective-permute-start.1 = (bf16[2,64,4096]{2,1,0:T(8,128)(2,1)S(1)}, bf16[2,64,4096]{2,1,0:T(8,128)(2,1)S(1)}, u32[]{:S(2)}, u32[]{:S(2)}) collective-permute-start(bf16[2,64,4096]{2,1,0:T(8,128)(2,1)S(1)} %get-tuple-element.92), channel_id=1, source_target_pairs={{2,0},{6,2},{10,4},{14,6},{18,8},{22,10},{26,12},{30,14},{28,16},{... | collective-permute-start | bytes 3145736 | tf_op jit(solution)/shard_map/ppermute | solution.py:458
  45.8 24.3 %collective-permute-start.9 = (bf16[128,4096]{1,0:T(8,128)(2,1)S(1)}, bf16[128,4096]{1,0:T(8,128)(2,1)S(1)}, u32[]{:S(2)}, u32[]{:S(2)}) collective-permute-start(bf16[128,4096]{1,0:T(8,128)(2,1)S(1)} %input.8.rest_0_.own_ref.refs_1_), channel_id=1, source_target_pairs={{0,2},{2,4},{4,6},{6,8},{8,10},{10,12},{12,14},{14,16},{16,18},{18... | collective-permute-start | bytes 3145736 | tf_op jit(solution)/shard_map/ppermute | solution.py:393
  70.1 4.4 %forward.5 = (bf16[128,4096]{1,0:T(8,128)(2,1)S(1)}, bf16[128,4096]{1,0:T(8,128)(2,1)S(1)}, f32[8,128]{1,0:T(8,128)S(1)}) custom-call(bf16[3,256,128]{2,1,0:T(8,128)(2,1)S(1)} %copy-done.5, bf16[128,4096]{1,0:T(8,128)(2,1)S(1)} %copy-done.7, bf16[128,4096]{1,0:T(8,128)(2,1)S(1)} %collective-permute-done.3.halo_ref.refs_5_, ...), custom_call_target="tpu_custom_call" | custom-call | flops 1 | bytes 1 | tf_op jit(solution)/shard_map/forward/pallas_call | solution.py:367
  79.0 4.4 %collective-permute-start.8 = (bf16[128,4096]{1,0:T(8,128)(2,1)S(1)}, bf16[128,4096]{1,0:T(8,128)(2,1)S(1)}, u32[]{:S(2)}, u32[]{:S(2)}) collective-permute-start(bf16[128,4096]{1,0:T(8,128)(2,1)S(1)} %input.9.rest_0_.own_ref.refs_4_), channel_id=1, source_target_pairs={{0,2},{2,4},{4,6},{6,8},{8,10},{10,12},{12,14},{14,16},{16,18},{18... | collective-permute-start | bytes 3145736 | tf_op jit(solution)/shard_map/ppermute | solution.py:393
  87.2 4.4 %forward.6 = (bf16[128,4096]{1,0:T(8,128)(2,1)S(1)}, bf16[128,4096]{1,0:T(8,128)(2,1)S(1)}, f32[8,128]{1,0:T(8,128)S(1)}) custom-call(bf16[3,256,128]{2,1,0:T(8,128)(2,1)S(1)} %copy-done.5, bf16[128,4096]{1,0:T(8,128)(2,1)S(1)} %input.8.rest_0_.own_ref.refs_1_, bf16[128,4096]{1,0:T(8,128)(2,1)S(1)} %collective-permute-done.9.halo_ref.refs_2_, ...), custom_call_target="tpu_custom_call" | custom-call | flops 1 | bytes 1 | tf_op jit(solution)/shard_map/forward/pallas_call | solution.py:367
  96.1 4.4 %forward.7 = (bf16[128,4096]{1,0:T(8,128)(2,1)S(1)}, bf16[128,4096]{1,0:T(8,128)(2,1)S(1)}, f32[8,128]{1,0:T(8,128)S(1)}) custom-call(bf16[3,256,128]{2,1,0:T(8,128)(2,1)S(1)} %copy-done.5, bf16[128,4096]{1,0:T(8,128)(2,1)S(1)} %input.9.rest_0_.own_ref.refs_4_, bf16[128,4096]{1,0:T(8,128)(2,1)S(1)} %collective-permute-done.8.halo_ref.refs_5_, ...), custom_call_target="tpu_custom_call" | custom-call | flops 1 | bytes 1 | tf_op jit(solution)/shard_map/forward/pallas_call | solution.py:367
  105.0 4.7 %backward.6 = (bf16[3,2,128,4096]{3,2,1,0:T(8,128)(2,1)}, bf16[128,4096]{1,0:T(8,128)(2,1)S(1)}, f32[8,128]{1,0:T(8,128)S(1)}) custom-call(bf16[3,256,128]{2,1,0:T(8,128)(2,1)S(1)} %copy-done.5, bf16[128,4096]{1,0:T(8,128)(2,1)S(1)} %gate.2.rest_0_.own_ref.refs_0_, bf16[128,4096]{1,0:T(8,128)(2,1)S(1)} %collective-permute-done.12.halo_ref, ...), custom_call_target="tpu_custom_call" | custom-call | flops 1 | bytes 1 | tf_op jit(solution)/shard_map/backward/pallas_call | solution.py:367
  111.2 23.5 %collective-permute-start.18 = (bf16[128,4096]{1,0:T(8,128)(2,1)S(1)}, bf16[128,4096]{1,0:T(8,128)(2,1)S(1)}, u32[]{:S(2)}, u32[]{:S(2)}) collective-permute-start(bf16[128,4096]{1,0:T(8,128)(2,1)S(1)} %input.10.rest_0_.own_ref.refs_1_), channel_id=1, source_target_pairs={{0,2},{2,4},{4,6},{6,8},{8,10},{10,12},{12,14},{14,16},{16,18},{18... | collective-permute-start | bytes 3145736 | tf_op jit(solution)/shard_map/ppermute | solution.py:393
  134.7 5.8 %collective-permute-start.17 = (bf16[128,4096]{1,0:T(8,128)(2,1)S(1)}, bf16[128,4096]{1,0:T(8,128)(2,1)S(1)}, u32[]{:S(2)}, u32[]{:S(2)}) collective-permute-start(bf16[128,4096]{1,0:T(8,128)(2,1)S(1)} %input.11.rest_0_.own_ref.refs_4_), channel_id=1, source_target_pairs={{0,2},{2,4},{4,6},{6,8},{8,10},{10,12},{12,14},{14,16},{16,18},{18... | collective-permute-start | bytes 3145736 | tf_op jit(solution)/shard_map/ppermute | solution.py:393
  144.3 4.7 %backward.7 = (bf16[3,2,128,4096]{3,2,1,0:T(8,128)(2,1)}, bf16[128,4096]{1,0:T(8,128)(2,1)S(1)}, f32[8,128]{1,0:T(8,128)S(1)}) custom-call(bf16[3,256,128]{2,1,0:T(8,128)(2,1)S(1)} %copy-done.5, bf16[128,4096]{1,0:T(8,128)(2,1)S(1)} %gate.3.rest_0_.own_ref.refs_3_, ...), custom_call_target="tpu_custom_call", output_to_operand_aliasing={{0}: (7, {})} | custom-call | flops 1 | bytes 1 | tf_op jit(solution)/shard_map/backward/pallas_call | solution.py:367
  156.9 4.7 %last_forward.2.rest_0_ = bf16[3,2,128,4096]{3,2,1,0:T(8,128)(2,1)} custom-call(bf16[3,256,128]{2,1,0:T(8,128)(2,1)S(1)} %copy-done.5, bf16[128,4096]{1,0:T(8,128)(2,1)S(1)} %input.10.rest_0_.own_ref.refs_1_, bf16[128,4096]{1,0:T(8,128)(2,1)S(1)} %collective-permute-done.18.halo_ref.refs_2_, ...), custom_call_target="tpu_custom_call", output_to_operand_aliasing={{}: (6, {})} | custom-call | flops 1 | bytes 1 | tf_op jit(solution)/shard_map/last_forward/pallas_call | solution.py:367
  161.6 4.7 %last_forward.3.rest_0_.rest_1_ = bf16[3,2,128,4096]{3,2,1,0:T(8,128)(2,1)} custom-call(bf16[3,256,128]{2,1,0:T(8,128)(2,1)S(1)} %copy-done.5, bf16[128,4096]{1,0:T(8,128)(2,1)S(1)} %input.11.rest_0_.own_ref.refs_4_, bf16[128,4096]{1,0:T(8,128)(2,1)S(1)} %collective-permute-done.17.halo_ref.refs_5_, ...), custom_call_target="tpu_custom_call", output_to_operand_aliasing={{}: (5, {})} | custom-call | flops 1 | bytes 1 | tf_op jit(solution)/shard_map/last_forward/pallas_call | solution.py:367
  169.0 4.7 %backward.8 = (bf16[3,2,128,4096]{3,2,1,0:T(8,128)(2,1)}, bf16[128,4096]{1,0:T(8,128)(2,1)S(1)}, f32[8,128]{1,0:T(8,128)S(1)}) custom-call(bf16[3,256,128]{2,1,0:T(8,128)(2,1)S(1)} %copy-done.5, bf16[128,4096]{1,0:T(8,128)(2,1)S(1)} %copy-done.16, bf16[128,4096]{1,0:T(8,128)(2,1)S(1)} %collective-permute-done.16.halo_ref, ...), custom_call_target="tpu_custom_call", output_to_operand_aliasing={{0}: (7, {})} | custom-call | flops 1 | bytes 1 | tf_op jit(solution)/shard_map/backward/pallas_call | solution.py:367
  181.2 5.6 %backward.9 = (bf16[3,2,128,4096]{3,2,1,0:T(8,128)(2,1)}, bf16[128,4096]{1,0:T(8,128)(2,1)S(1)}, f32[8,128]{1,0:T(8,128)S(1)}) custom-call(bf16[3,256,128]{2,1,0:T(8,128)(2,1)S(1)} %copy-done.5, bf16[128,4096]{1,0:T(8,128)(2,1)} %get-tuple-element.63.rest_0_.own_ref.refs_3_, ...), custom_call_target="tpu_custom_call", output_to_operand_aliasing={{0}: (7, {})} | custom-call | flops 1 | bytes 1 | tf_op jit(solution)/shard_map/backward/pallas_call | solution.py:367
  194.9 7.0 %taps.3.refs_6_.refs_2_ = f32[128,256]{1,0:T(8,128)S(1)} custom-call(bf16[128,4096]{1,0:T(8,128)(2,1)S(1)} %gate.2.rest_0_.own_ref.refs_0_, bf16[128,4096]{1,0:T(8,128)(2,1)S(1)} %input.10.rest_0_.own_ref.refs_1_, bf16[128,4096]{1,0:T(8,128)(2,1)S(1)} %copy-done.26, bf16[128,4096]{1,0:T(8,128)(2,1)S(1)} %gate.3.rest_0_.own_ref.refs_3_, ...), custom_call_target="tpu_custom_call" | custom-call | flops 1 | bytes 1 | tf_op jit(solution)/shard_map/taps/pallas_call | solution.py:367
  201.9 7.9 %taps.4.refs_6_.refs_1_ = f32[128,256]{1,0:T(8,128)S(1)} custom-call(bf16[128,4096]{1,0:T(8,128)(2,1)S(1)} %copy-done.16, bf16[128,4096]{1,0:T(8,128)(2,1)S(1)} %input.8.rest_0_.own_ref.refs_1_, bf16[128,4096]{1,0:T(8,128)(2,1)S(1)} %copy-done.22, bf16[128,4096]{1,0:T(8,128)(2,1)} %get-tuple-element.63.rest_0_.own_ref.refs_3_, ...), custom_call_target="tpu_custom_call" | custom-call | flops 1 | bytes 1 | tf_op jit(solution)/shard_map/taps/pallas_call | solution.py:367
  209.8 7.7 %taps.5.rest_0_.refs_0_ = f32[128,256]{1,0:T(8,128)S(1)} custom-call(bf16[128,4096]{1,0:T(8,128)(2,1)S(1)} %get-tuple-element.69.rest_0_.refs_0_.own_ref, bf16[128,4096]{1,0:T(8,128)(2,1)S(1)} %copy-done.6, bf16[128,4096]{1,0:T(8,128)(2,1)S(1)} %copy-done.18, bf16[128,4096]{1,0:T(8,128)(2,1)} %get-tuple-element.75.refs_6_.refs_3_.own_ref, ...), custom_call_target="tpu_custom_call" | custom-call | flops 1 | bytes 1 | tf_op jit(solution)/shard_map/taps/pallas_call | solution.py:367
  217.6 4.7 %backward.10 = (bf16[3,2,128,4096]{3,2,1,0:T(8,128)(2,1)}, bf16[128,4096]{1,0:T(8,128)(2,1)S(1)}, f32[8,128]{1,0:T(8,128)S(1)}) custom-call(bf16[3,256,128]{2,1,0:T(8,128)(2,1)S(1)} %copy-done.5, bf16[128,4096]{1,0:T(8,128)(2,1)S(1)} %get-tuple-element.69.rest_0_.refs_0_.own_ref, ...), custom_call_target="tpu_custom_call", output_to_operand_aliasing={{0}: (7, {})} | custom-call | flops 1 | bytes 1 | tf_op jit(solution)/shard_map/backward/pallas_call | solution.py:367
  232.2 38.3 %all-to-all-start = ((f32[3,128,256]{2,0,1:T(4,128)}), f32[3,128,256]{2,0,1:T(4,128)}, u32[]{:S(2)}, u32[]{:S(2)}) async-start(f32[3,128,256]{2,0,1:T(4,128)} %copy.21), calls=%async_computation | async-start | bytes 1048576 | tf_op jit(solution)/shard_map/all_to_all | solution.py:577
  273.3 5.8 %backward.11 = (bf16[3,2,128,4096]{3,2,1,0:T(8,128)(2,1)}, bf16[128,4096]{1,0:T(8,128)(2,1)S(1)}, f32[8,128]{1,0:T(8,128)S(1)}) custom-call(bf16[3,256,128]{2,1,0:T(8,128)(2,1)S(1)} %copy-done.5, bf16[128,4096]{1,0:T(8,128)(2,1)} %get-tuple-element.75.refs_6_.refs_3_.own_ref, ...), custom_call_target="tpu_custom_call", output_to_operand_aliasing={{0}: (7, {})} | custom-call | flops 1 | bytes 1 | tf_op jit(solution)/shard_map/backward/pallas_call | solution.py:367
  284.3 5.4 %collective-permute-start.26 = (bf16[64,4096]{1,0:T(8,128)(2,1)S(1)}, bf16[64,4096]{1,0:T(8,128)(2,1)S(1)}, u32[]{:S(2)}, u32[]{:S(2)}) collective-permute-start(bf16[64,4096]{1,0:T(8,128)(2,1)S(1)} %get-tuple-element.84.rest_0_), channel_id=1, source_target_pairs={{0,2},{2,6},{4,10},{6,14},{8,18},{10,22},{12,26},{14,30},{16,28},{... | collective-permute-start | bytes 1572872 | tf_op jit(solution)/shard_map/ppermute | solution.py:515
  289.7 8.2 %collective-permute-done.28.second_ref = bf16[64,4096]{1,0:T(8,128)(2,1)S(1)} collective-permute-done((bf16[64,4096]{1,0:T(8,128)(2,1)S(1)}, bf16[64,4096]{1,0:T(8,128)(2,1)S(1)}, u32[]{:S(2)}, u32[]{:S(2)}) %collective-permute-start.28) | collective-permute-done | bytes 524320 | tf_op jit(solution)/shard_map/ppermute | solution.py:515
  299.5 20.8 %collective-permute-done.26.second_ref = bf16[64,4096]{1,0:T(8,128)(2,1)S(1)} collective-permute-done((bf16[64,4096]{1,0:T(8,128)(2,1)S(1)}, bf16[64,4096]{1,0:T(8,128)(2,1)S(1)}, u32[]{:S(2)}, u32[]{:S(2)}) %collective-permute-start.26) | collective-permute-done | bytes 524320 | tf_op jit(solution)/shard_map/ppermute | solution.py:515
  (169 shorter events, 103.9 us)
Async XLA Ops:
  3.9 4.8 %collective-permute-start.2 = (f32[16,128]{1,0:T(8,128)}, f32[16,128]{1,0:T(8,128)S(1)}, u32[]{:S(2)}, u32[]{:S(2)}) collective-permute-start(f32[16,128]{1,0:T(8,128)} %squares.1.rest_0_), channel_id=1, source_target_pairs={{0,1},{1,0},{2,3},{3,2},{4,5},{5,4},{6,7},{7,6},{8,9},{9,8},{10,11... | collective-permute-start | bytes 24584 | tf_op jit(solution)/shard_map/ppermute | solution.py:398
  17.7 15.1 %collective-permute-start.4 = (bf16[128,4096]{1,0:T(8,128)(2,1)S(1)}, bf16[128,4096]{1,0:T(8,128)(2,1)S(1)}, u32[]{:S(2)}, u32[]{:S(2)}) collective-permute-start(bf16[128,4096]{1,0:T(8,128)(2,1)S(1)} %copy-done.6), channel_id=1, source_target_pairs={{0,2},{2,4},{4,6},{6,8},{8,10},{10,12},{12,14},{14,16},{16,18},{18... | collective-permute-start | bytes 3145736 | tf_op jit(solution)/shard_map/ppermute | solution.py:393
  19.4 50.7 %collective-permute-start.3 = (bf16[128,4096]{1,0:T(8,128)(2,1)}, bf16[128,4096]{1,0:T(8,128)(2,1)S(1)}, u32[]{:S(2)}, u32[]{:S(2)}) collective-permute-start(bf16[128,4096]{1,0:T(8,128)(2,1)} %input.7.rest_0_.own_ref.refs_4_), channel_id=1, source_target_pairs={{0,2},{2,4},{4,6},{6,8},{8,10},{10,12},{12,14},{14,16},{16,18},{18... | collective-permute-start | bytes 3145736 | tf_op jit(solution)/shard_map/ppermute | solution.py:393
  24.2 59.2 %collective-permute-start = (bf16[2,64,4096]{2,1,0:T(8,128)(2,1)S(1)}, bf16[2,64,4096]{2,1,0:T(8,128)(2,1)S(1)}, u32[]{:S(2)}, u32[]{:S(2)}) collective-permute-start(bf16[2,64,4096]{2,1,0:T(8,128)(2,1)S(1)} %get-tuple-element.93), channel_id=1, source_target_pairs={{0,0},{4,2},{8,4},{12,6},{16,8},{20,10},{24,12},{28,14},{30,16},{2... | collective-permute-start | bytes 3145736 | tf_op jit(solution)/shard_map/ppermute | solution.py:458
  25.0 58.5 %collective-permute-start.1 = (bf16[2,64,4096]{2,1,0:T(8,128)(2,1)S(1)}, bf16[2,64,4096]{2,1,0:T(8,128)(2,1)S(1)}, u32[]{:S(2)}, u32[]{:S(2)}) collective-permute-start(bf16[2,64,4096]{2,1,0:T(8,128)(2,1)S(1)} %get-tuple-element.92), channel_id=1, source_target_pairs={{2,0},{6,2},{10,4},{14,6},{18,8},{22,10},{26,12},{30,14},{28,16},{... | collective-permute-start | bytes 3145736 | tf_op jit(solution)/shard_map/ppermute | solution.py:458
  41.3 3.7 %collective-permute-start.5 = (f32[8,128]{1,0:T(8,128)S(1)}, f32[8,128]{1,0:T(8,128)S(1)}, u32[]{:S(2)}, u32[]{:S(2)}) collective-permute-start(f32[8,128]{1,0:T(8,128)S(1)} %get-tuple-element.47.rest_0_), channel_id=1, source_target_pairs={{0,1},{1,0},{2,3},{3,2},{4,5},{5,4},{6,7},{7,6},{8,9},{9,8},{10,11... | collective-permute-start | bytes 12296 | tf_op jit(solution)/shard_map/ppermute | solution.py:398
  45.8 41.4 %collective-permute-start.9 = (bf16[128,4096]{1,0:T(8,128)(2,1)S(1)}, bf16[128,4096]{1,0:T(8,128)(2,1)S(1)}, u32[]{:S(2)}, u32[]{:S(2)}) collective-permute-start(bf16[128,4096]{1,0:T(8,128)(2,1)S(1)} %input.8.rest_0_.own_ref.refs_1_), channel_id=1, source_target_pairs={{0,2},{2,4},{4,6},{6,8},{8,10},{10,12},{12,14},{14,16},{16,18},{18... | collective-permute-start | bytes 3145736 | tf_op jit(solution)/shard_map/ppermute | solution.py:393
  74.5 3.7 %collective-permute-start.6 = (f32[8,128]{1,0:T(8,128)S(1)}, f32[8,128]{1,0:T(8,128)S(1)}, u32[]{:S(2)}, u32[]{:S(2)}) collective-permute-start(f32[8,128]{1,0:T(8,128)S(1)} %get-tuple-element.49.rest_0_), channel_id=1, source_target_pairs={{0,1},{1,0},{2,3},{3,2},{4,5},{5,4},{6,7},{7,6},{8,9},{9,8},{10,11... | collective-permute-start | bytes 12296 | tf_op jit(solution)/shard_map/ppermute | solution.py:398
  79.0 17.1 %collective-permute-start.8 = (bf16[128,4096]{1,0:T(8,128)(2,1)S(1)}, bf16[128,4096]{1,0:T(8,128)(2,1)S(1)}, u32[]{:S(2)}, u32[]{:S(2)}) collective-permute-start(bf16[128,4096]{1,0:T(8,128)(2,1)S(1)} %input.9.rest_0_.own_ref.refs_4_), channel_id=1, source_target_pairs={{0,2},{2,4},{4,6},{6,8},{8,10},{10,12},{12,14},{14,16},{16,18},{18... | collective-permute-start | bytes 3145736 | tf_op jit(solution)/shard_map/ppermute | solution.py:393
  84.0 21.0 %collective-permute-start.12 = (bf16[128,4096]{1,0:T(8,128)(2,1)S(1)}, bf16[128,4096]{1,0:T(8,128)(2,1)S(1)}, u32[]{:S(2)}, u32[]{:S(2)}) collective-permute-start(bf16[128,4096]{1,0:T(8,128)(2,1)S(1)} %gate.2.rest_0_.own_ref.refs_0_), channel_id=1, source_target_pairs={{2,0},{4,2},{6,4},{8,6},{10,8},{12,10},{14,12},{16,14},{18,16},{20... | collective-permute-start | bytes 3145736 | tf_op jit(solution)/shard_map/ppermute | solution.py:393
  85.9 58.4 %collective-permute-start.7 = (bf16[128,4096]{1,0:T(8,128)(2,1)S(1)}, bf16[128,4096]{1,0:T(8,128)(2,1)S(1)}, u32[]{:S(2)}, u32[]{:S(2)}) collective-permute-start(bf16[128,4096]{1,0:T(8,128)(2,1)S(1)} %gate.3.rest_0_.own_ref.refs_3_), channel_id=1, source_target_pairs={{2,0},{4,2},{6,4},{8,6},{10,8},{12,10},{14,12},{16,14},{18,16},{20... | collective-permute-start | bytes 3145736 | tf_op jit(solution)/shard_map/ppermute | solution.py:393
  91.6 3.7 %collective-permute-start.10 = (f32[8,128]{1,0:T(8,128)S(1)}, f32[8,128]{1,0:T(8,128)S(1)}, u32[]{:S(2)}, u32[]{:S(2)}) collective-permute-start(f32[8,128]{1,0:T(8,128)S(1)} %get-tuple-element.51.rest_0_), channel_id=1, source_target_pairs={{0,1},{1,0},{2,3},{3,2},{4,5},{5,4},{6,7},{7,6},{8,9},{9,8},{10,11... | collective-permute-start | bytes 12296 | tf_op jit(solution)/shard_map/ppermute | solution.py:398
  100.5 3.7 %collective-permute-start.11 = (f32[8,128]{1,0:T(8,128)S(1)}, f32[8,128]{1,0:T(8,128)S(1)}, u32[]{:S(2)}, u32[]{:S(2)}) collective-permute-start(f32[8,128]{1,0:T(8,128)S(1)} %get-tuple-element.52.rest_0_), channel_id=1, source_target_pairs={{0,1},{1,0},{2,3},{3,2},{4,5},{5,4},{6,7},{7,6},{8,9},{9,8},{10,11... | collective-permute-start | bytes 12296 | tf_op jit(solution)/shard_map/ppermute | solution.py:398
  109.7 30.8 %collective-permute-start.13 = (f32[8,128]{1,0:T(8,128)S(1)}, f32[8,128]{1,0:T(8,128)S(1)}, u32[]{:S(2)}, u32[]{:S(2)}) collective-permute-start(f32[8,128]{1,0:T(8,128)S(1)} %get-tuple-element.55.rest_0_), channel_id=1, source_target_pairs={{0,1},{1,0},{2,3},{3,2},{4,5},{5,4},{6,7},{7,6},{8,9},{9,8},{10,11... | collective-permute-start | bytes 12296 | tf_op jit(solution)/shard_map/ppermute | solution.py:398
  111.2 45.7 %collective-permute-start.18 = (bf16[128,4096]{1,0:T(8,128)(2,1)S(1)}, bf16[128,4096]{1,0:T(8,128)(2,1)S(1)}, u32[]{:S(2)}, u32[]{:S(2)}) collective-permute-start(bf16[128,4096]{1,0:T(8,128)(2,1)S(1)} %input.10.rest_0_.own_ref.refs_1_), channel_id=1, source_target_pairs={{0,2},{2,4},{4,6},{6,8},{8,10},{10,12},{12,14},{14,16},{16,18},{18... | collective-permute-start | bytes 3145736 | tf_op jit(solution)/shard_map/ppermute | solution.py:393
  134.7 26.9 %collective-permute-start.17 = (bf16[128,4096]{1,0:T(8,128)(2,1)S(1)}, bf16[128,4096]{1,0:T(8,128)(2,1)S(1)}, u32[]{:S(2)}, u32[]{:S(2)}) collective-permute-start(bf16[128,4096]{1,0:T(8,128)(2,1)S(1)} %input.11.rest_0_.own_ref.refs_4_), channel_id=1, source_target_pairs={{0,2},{2,4},{4,6},{6,8},{8,10},{10,12},{12,14},{14,16},{16,18},{18... | collective-permute-start | bytes 3145736 | tf_op jit(solution)/shard_map/ppermute | solution.py:393
  143.0 23.2 %collective-permute-start.16 = (bf16[128,4096]{1,0:T(8,128)(2,1)S(1)}, bf16[128,4096]{1,0:T(8,128)(2,1)S(1)}, u32[]{:S(2)}, u32[]{:S(2)}) collective-permute-start(bf16[128,4096]{1,0:T(8,128)(2,1)S(1)} %get-tuple-element.57.rest_0_.own_ref.refs_0_), channel_id=1, source_target_pairs={{2,0},{4,2},{6,4},{8,6},{10,8},{12,10},{14,12},{16,14},{18,16},{20... | collective-permute-start | bytes 3145736 | tf_op jit(solution)/shard_map/ppermute | solution.py:393
  155.4 25.8 %collective-permute-start.15 = (bf16[128,4096]{1,0:T(8,128)(2,1)}, bf16[128,4096]{1,0:T(8,128)(2,1)S(1)}, u32[]{:S(2)}, u32[]{:S(2)}) collective-permute-start(bf16[128,4096]{1,0:T(8,128)(2,1)} %get-tuple-element.63.rest_0_.own_ref.refs_3_), channel_id=1, source_target_pairs={{2,0},{4,2},{6,4},{8,6},{10,8},{12,10},{14,12},{16,14},{18,16},{20... | collective-permute-start | bytes 3145736 | tf_op jit(solution)/shard_map/ppermute | solution.py:393
  179.9 37.7 %collective-permute-start.22 = (bf16[128,4096]{1,0:T(8,128)(2,1)S(1)}, bf16[128,4096]{1,0:T(8,128)(2,1)S(1)}, u32[]{:S(2)}, u32[]{:S(2)}) collective-permute-start(bf16[128,4096]{1,0:T(8,128)(2,1)S(1)} %get-tuple-element.69.rest_0_.refs_0_.own_ref), channel_id=1, source_target_pairs={{2,0},{4,2},{6,4},{8,6},{10,8},{12,10},{14,12},{16,14},{18,16},{20... | collective-permute-start | bytes 3145736 | tf_op jit(solution)/shard_map/ppermute | solution.py:393
  193.3 77.2 %collective-permute-start.21 = (bf16[128,4096]{1,0:T(8,128)(2,1)}, bf16[128,4096]{1,0:T(8,128)(2,1)}, u32[]{:S(2)}, u32[]{:S(2)}) collective-permute-start(bf16[128,4096]{1,0:T(8,128)(2,1)} %get-tuple-element.75.refs_6_.refs_3_.own_ref), channel_id=1, source_target_pairs={{2,0},{4,2},{6,4},{8,6},{10,8},{12,10},{14,12},{16,14},{18,16},{20... | collective-permute-start | bytes 3145736 | tf_op jit(solution)/shard_map/ppermute | solution.py:393
  232.2 89.8 %all-to-all-start = ((f32[3,128,256]{2,0,1:T(4,128)}), f32[3,128,256]{2,0,1:T(4,128)}, u32[]{:S(2)}, u32[]{:S(2)}) async-start(f32[3,128,256]{2,0,1:T(4,128)} %copy.21), calls=%async_computation | async-start | bytes 1048576 | tf_op jit(solution)/shard_map/all_to_all | solution.py:577
  280.1 17.8 %collective-permute-start.28 = (bf16[64,4096]{1,0:T(8,128)(2,1)S(1)}, bf16[64,4096]{1,0:T(8,128)(2,1)S(1)}, u32[]{:S(2)}, u32[]{:S(2)}) collective-permute-start(bf16[64,4096]{1,0:T(8,128)(2,1)S(1)} %get-tuple-element.79.rest_0_), channel_id=1, source_target_pairs={{0,2},{2,6},{4,10},{6,14},{8,18},{10,22},{12,26},{14,30},{16,28},{... | collective-permute-start | bytes 1572872 | tf_op jit(solution)/shard_map/ppermute | solution.py:515
  283.6 15.9 %collective-permute-start.25 = (bf16[64,4096]{1,0:T(8,128)(2,1)S(1)}, bf16[64,4096]{1,0:T(8,128)(2,1)S(1)}, u32[]{:S(2)}, u32[]{:S(2)}) collective-permute-start(bf16[64,4096]{1,0:T(8,128)(2,1)S(1)} %get-tuple-element.83), channel_id=1, source_target_pairs={{0,0},{2,4},{4,8},{6,12},{8,16},{10,20},{12,24},{14,28},{16,30},{1... | collective-permute-start | bytes 1572872 | tf_op jit(solution)/shard_map/ppermute | solution.py:515
  284.3 36.1 %collective-permute-start.26 = (bf16[64,4096]{1,0:T(8,128)(2,1)S(1)}, bf16[64,4096]{1,0:T(8,128)(2,1)S(1)}, u32[]{:S(2)}, u32[]{:S(2)}) collective-permute-start(bf16[64,4096]{1,0:T(8,128)(2,1)S(1)} %get-tuple-element.84.rest_0_), channel_id=1, source_target_pairs={{0,2},{2,6},{4,10},{6,14},{8,18},{10,22},{12,26},{14,30},{16,28},{... | collective-permute-start | bytes 1572872 | tf_op jit(solution)/shard_map/ppermute | solution.py:515
  (48 other events, 526.0 us)
